TPU v7x, 32 devices: a whole 2x2x4 slice. The times are simulated.
32 devices in a mesh: depth: 4 (over z), row: 8 (over y, x, core).
Axes of the slice: x: 2, y: 2, z: 4, core: 2. Of those that a mesh axis runs over, the one named last changes fastest.
Arguments:
- volume: float32 [128, 256, 4096], P('depth', 'row'), may hold values from 0.02 to 0.52
- palette: float32 [3, 8], replicated, may hold values from 0.15 to 4
Outputs:
- image: float32 [4, 256, 4096], P(None, 'row', 'depth')
All inputs are finite; a program needn't handle non-finite values.
Results may differ from a plain program's by a relative error of at most 0.0003.
Values sent between devices are 32-bit elements; how exact they have to be, the bound alone decides.
A program may use at most 192 MiB of HBM per device.

v0:
```python
import jax
import jax.numpy as jnp
from jax import lax
from jax.sharding import PartitionSpec as P


def padded_2(cells, sides, width):
    for axis, dim in sides:
        count = lax.axis_size(axis)
        ends = count - 1
        head = lax.slice_in_dim(cells, 0, width, axis=dim)
        tail = lax.slice_in_dim(cells, cells.shape[dim] - width, cells.shape[dim], axis=dim)
        cells = jnp.concatenate(
            [
                lax.ppermute(tail, axis, [(i, (i + 1) % count) for i in range(ends)]),
                cells,
                lax.ppermute(head, axis, [((i + 1) % count, i) for i in range(ends)]),
            ],
            axis=dim,
        )
    return cells


def swapped(value, axis, stride):
    mask = 2**stride
    pairs = [(source, source ^ mask) for source in range(lax.axis_size(axis))]
    return lax.ppermute(value, axis, pairs)


def sample_terms(field, grad_z, grad_y, grad_x, palette, scale):
    along = 0.36 * grad_z + 0.48 * grad_y + 0.8 * grad_x
    square = grad_z * grad_z + grad_y * grad_y + grad_x * grad_x
    shade = 0.25 + 0.75 * jnp.abs(along) / jnp.sqrt(square + 0.04)
    bumps = palette.shape[1]
    colors = [jnp.zeros_like(field) for k in range(3)]
    for j in range(bumps):
        bump = jnp.exp(-jnp.square((bumps - 1) * field - j))
        for k in range(3):
            colors[k] = colors[k] + palette[k, j] * bump
    colors = [shade * c for c in colors]
    return (field * scale, colors)


def over_blend(front, back):
    color = front[:3] + front[3:4] * back[:3]
    passed = front[3:4] * back[3:4]
    return jnp.concatenate([color, passed], axis=0)


def on_device(volume, palette):
    depth_cells, rows, columns = volume.shape
    groups = lax.axis_size("depth")
    scale = 4.0 / (depth_cells * groups)
    padded = padded_2(volume, (("depth", 0), ("row", 1)), 1)
    grad_z = (padded[2:, 1:-1, :] - padded[:-2, 1:-1, :]) * 0.5
    grad_y = (padded[1:-1, 2:, :] - padded[1:-1, :-2, :]) * 0.5
    side_pad = jnp.pad(volume, ((0, 0), (0, 0), (1, 1)))
    grad_x = (side_pad[:, :, 2:] - side_pad[:, :, :-2]) * 0.5
    tau, colors = sample_terms(volume, grad_z, grad_y, grad_x, palette, scale)
    before = jnp.cumsum(tau, axis=0) - tau
    weight = jnp.exp(-before) * (1.0 - jnp.exp(-tau))
    channels = [jnp.sum(weight * c, axis=0) for c in colors]
    channels.append(jnp.exp(-jnp.sum(tau, axis=0)))
    partial_image = jnp.stack(channels, axis=0)
    block_width = columns // groups
    piece = partial_image.reshape(4, rows, groups, block_width)
    index = lax.axis_index("depth")
    for bit in range(groups.bit_length() - 1):
        mine = index // 2**bit % 2
        paired = piece.reshape(4, rows, piece.shape[2] // 2, 2, block_width)
        first = paired[:, :, :, 0, :]
        second = paired[:, :, :, 1, :]
        keep = jnp.where(mine == 0, first, second)
        outgoing = jnp.where(mine == 0, second, first)
        arrived = swapped(outgoing, "depth", bit)
        front = jnp.where(mine == 0, keep, arrived)
        back = jnp.where(mine == 0, arrived, keep)
        piece = over_blend(front, back)
    final = piece[:, :, 0, :]
    return jnp.concatenate([final[:3], 1.0 - final[3:4]], axis=0)


def solution(mesh):
    return jax.shard_map(
        on_device,
        mesh=mesh,
        in_specs=(P("depth", "row", None), P()),
        out_specs=P(None, "row", "depth"),
        check_vma=False,
    )
```

profile of v0, /device:TPU:11, one launch (start us, length us, event | category | flops | bytes accessed | tf_op | source)
XLA Modules:
  0.0 228.5 jit_solution(13457746965545198184)
XLA Ops:
  0.0 1.3 fusion.16
  1.3 3.2 %collective-permute-start.1 = (f32[1,32,4096]{2,1,0:T(8,128)S(1)}, f32[1,32,4096]{2,1,0:T(8,128)S(1)}, u32[]{:S(2)}, u32[]{:S(2)}) collective-permute-start(f32[1,32,4096]{2,1,0:T(8,128)S(1)} %get-tuple-element.12), channel_id=1, source_target_pairs={{0,8},{8,16},{16,24},{1,9},{9,17},{17,25},{2,10},{10,18},{18,26},{... | collective-permute-start | bytes 1572872 | tf_op jit(solution)/shard_map/ppermute | solution.py:15
  4.5 2.1 collective-permute-start
  6.6 9.4 %collective-permute-done.1 = f32[1,32,4096]{2,1,0:T(8,128)S(1)} collective-permute-done((f32[1,32,4096]{2,1,0:T(8,128)S(1)}, f32[1,32,4096]{2,1,0:T(8,128)S(1)}, u32[]{:S(2)}, u32[]{:S(2)}) %collective-permute-start.1) | collective-permute-done | bytes 524320 | tf_op jit(solution)/shard_map/ppermute | solution.py:15
  16.0 0.0 copy-start.2
  16.0 7.4 %constant_dynamic-update-slice_fusion.1 = f32[34,32,4096]{2,1,0:T(8,128)S(1)} fusion(f32[34,32,4096]{2,1,0:T(8,128)S(1)} %constant_dynamic-update-slice_fusion.2, f32[32,32,4096]{2,1,0:T(8,128)} %param.2), kind=kLoop, calls=%fused_computation.50 | loop fusion | bytes 33554432
  23.4 0.0 collective-permute-done
  23.4 0.0 copy-start
  23.4 6.1 %copy-done = f32[34,32,4096]{2,1,0:T(8,128)} copy-done((f32[34,32,4096]{2,1,0:T(8,128)}, f32[34,32,4096]{2,1,0:T(8,128)S(1)}, u32[]{:S(2)}) %copy-start) | copy-done | bytes 17825816
  29.5 1.8 fusion.15
  31.4 3.4 %collective-permute-start.2 = (f32[34,1,4096]{2,1,0:T(1,128)}, f32[34,1,4096]{2,1,0:T(1,128)S(1)}, u32[]{:S(2)}, u32[]{:S(2)}) collective-permute-start(f32[34,1,4096]{2,1,0:T(1,128)} %get-tuple-element.9), channel_id=1, source_target_pairs={{1,0},{2,1},{3,2},{4,3},{5,4},{6,5},{7,6},{9,8},{10,9},{11,10},{12... | collective-permute-start | bytes 1671176 | tf_op jit(solution)/shard_map/ppermute | solution.py:17
  34.8 3.0 %collective-permute-start.3 = (f32[34,1,4096]{2,1,0:T(1,128)S(1)}, f32[34,1,4096]{2,1,0:T(1,128)S(1)}, u32[]{:S(2)}, u32[]{:S(2)}) collective-permute-start(f32[34,1,4096]{2,1,0:T(1,128)S(1)} %get-tuple-element.10), channel_id=1, source_target_pairs={{0,1},{1,2},{2,3},{3,4},{4,5},{5,6},{6,7},{8,9},{9,10},{10,11},{11... | collective-permute-start | bytes 1671176 | tf_op jit(solution)/shard_map/ppermute | solution.py:15
  37.9 0.0 copy-done.2
  37.9 0.7 fusion.20
  38.5 0.7 fusion.19
  39.3 7.4 %collective-permute-done.2 = f32[34,1,4096]{2,1,0:T(1,128)S(1)} collective-permute-done((f32[34,1,4096]{2,1,0:T(1,128)}, f32[34,1,4096]{2,1,0:T(1,128)S(1)}, u32[]{:S(2)}, u32[]{:S(2)}) %collective-permute-start.2) | collective-permute-done | bytes 557088 | tf_op jit(solution)/shard_map/ppermute | solution.py:17
  46.6 1.0 collective-permute-done.3
  47.6 0.0 copy-start.1
  47.6 0.8 copy-done.1
  48.5 79.4 %multiply_reduce_fusion = (f32[32,4096]{1,0:T(8,128)S(1)}, f32[32,4096]{1,0:T(8,128)S(1)}, f32[32,4096]{1,0:T(8,128)S(1)}, f32[32,32,4096]{2,1,0:T(8,128)}, f32[32,32,4096]{2,1,0:T(8,128)}) fusion(f32[32,32,4096]{2,1,0:T(8,128)} %param.2, f32[]{:T(128)} %bitcast.23, f32[]{:T(128)} %bitcast.22, f32[]{:T(128)} %bitcast.21, f32[]{:T(128)} %bitcast.20, ...), kind=kOutput, calls=%fused_computation.6 | output fusion | flops 519700480 | bytes 88678400 | tf_op jit(solution)/shard_map/jit(cumsum)/reduce_window_sum | solution.py:60
  127.8 35.3 %multiply_reduce_fusion.2 = f32[32,4096]{1,0:T(8,128)S(1)} fusion(f32[32,32,4096]{2,1,0:T(8,128)} %get-tuple-element.48, f32[32,32,4096]{2,1,0:T(8,128)} %get-tuple-element.8, f32[32,32,4096]{2,1,0:T(8,128)} %param.2, f32[]{:T(128)} %bitcast.7, f32[]{:T(128)} %bitcast.6, f32[]{:T(128)} %bitcast.5, f32[]{:T(128)} %bitcast.4, f32[]{:T(128)} %bitcast.3, ...), kind=kLoop, calls=%fused_computation.8 | loop fusion | flops 176029696 | bytes 50855968 | tf_op jit(solution)/shard_map/reduce_sum | solution.py:62
  163.2 0.4 stack.13
  163.6 0.8 constant_dynamic-update-slice_fusion.6
  164.4 0.4 stack.14
  164.9 0.4 stack.15
  165.3 0.1 negate_exponential_fusion.8
  165.4 0.4 exp.55
  165.9 0.8 constant_dynamic-update-slice_fusion.5
  166.7 0.8 constant_dynamic-update-slice_fusion.4
  167.5 0.8 constant_dynamic-update-slice_fusion.3
  168.4 4.4 %fusion.17 = (f32[4,32,2,1,1024]{4,3,2,1,0:T(1,128)S(1)}, f32[4,32,2,1,1024]{4,3,2,1,0:T(1,128)S(1)}, f32[4,32,2,1,1024]{4,3,2,1,0:T(1,128)S(1)}) fusion(f32[4,32,2,2,1024]{4,3,2,1,0:T(2,128)} %constant_dynamic-update-slice_fusion.3, pred[]{:T(512)S(6)} %eq.8), kind=kLoop, calls=%fused_computation.59 | loop fusion | flops 262144 | bytes 5242881 | tf_op jit(solution)/shard_map/slice | solution.py:71
  172.8 0.5 copy.34
  173.3 0.1 collective-permute-start.4
  173.4 23.4 %collective-permute-done.4 = f32[4,32,2,1024]{3,2,1,0:T(2,128)} collective-permute-done((f32[4,32,2,1024]{3,2,1,0:T(2,128)S(1)}, f32[4,32,2,1024]{3,2,1,0:T(2,128)}, u32[]{:S(2)}, u32[]{:S(2)}) %collective-permute-start.4) | collective-permute-done | bytes 1048608 | tf_op jit(solution)/shard_map/ppermute | solution.py:27
  196.9 2.4 %broadcast_select_fusion.2 = (f32[4,32,2,1024]{3,2,1,0:T(2,128)S(1)}, f32[4,32,2,1024]{3,2,1,0:T(2,128)S(1)}) fusion(f32[4,32,2,1024]{3,2,1,0:T(2,128)} %collective-permute-done.4, pred[]{:T(512)S(6)} %eq.8, f32[4,32,2,1,1024]{4,3,2,1,0:T(1,128)S(1)} %get-tuple-element.17, f32[4,32,2,1,1024]{4,3,2,1,0:T(1,128)S(1)} %get-tuple-element.15), kind=kLoop, calls=%fused_computation.30 | loop fusion | flops 786432 | bytes 5242881 | tf_op jit(solution)/shard_map/jit(_where)/select_n | solution.py:76
  199.3 0.2 slice_bitcast_fusion
  199.5 0.5 fusion.8
  200.0 0.5 maximum_bitcast_fusion
  200.5 0.5 fusion.10
  201.0 2.4 %collective-permute-start.5 = (f32[4,32,1,1024]{3,2,1,0:T(1,128)S(1)}, f32[4,32,1,1024]{3,2,1,0:T(1,128)S(1)}, u32[]{:S(2)}, u32[]{:S(2)}) collective-permute-start(f32[4,32,1,1024]{3,2,1,0:T(1,128)S(1)} %fusion.10), channel_id=1, source_target_pairs={{0,16},{8,24},{16,0},{24,8},{1,17},{9,25},{17,1},{25,9},{2,18},{10... | collective-permute-start | bytes 1572872 | tf_op jit(solution)/shard_map/ppermute | solution.py:27
  203.4 22.5 %collective-permute-done.5 = f32[4,32,1,1024]{3,2,1,0:T(1,128)S(1)} collective-permute-done((f32[4,32,1,1024]{3,2,1,0:T(1,128)S(1)}, f32[4,32,1,1024]{3,2,1,0:T(1,128)S(1)}, u32[]{:S(2)}, u32[]{:S(2)}) %collective-permute-start.5) | collective-permute-done | bytes 524320 | tf_op jit(solution)/shard_map/ppermute | solution.py:27
  225.9 0.9 broadcast_select_fusion.5
  226.8 0.2 fusion.18
  227.0 0.5 fusion.11
  227.5 0.1 copy.35
  227.6 0.8 pad_maximum_fusion.4
  (4 shorter events, 0.1 us)
Async XLA Ops:
  1.3 14.7 %collective-permute-start.1 = (f32[1,32,4096]{2,1,0:T(8,128)S(1)}, f32[1,32,4096]{2,1,0:T(8,128)S(1)}, u32[]{:S(2)}, u32[]{:S(2)}) collective-permute-start(f32[1,32,4096]{2,1,0:T(8,128)S(1)} %get-tuple-element.12), channel_id=1, source_target_pairs={{0,8},{8,16},{16,24},{1,9},{9,17},{17,25},{2,10},{10,18},{18,26},{... | collective-permute-start | bytes 1572872 | tf_op jit(solution)/shard_map/ppermute | solution.py:15
  4.5 18.9 %collective-permute-start = (f32[1,32,4096]{2,1,0:T(8,128)S(1)}, f32[1,32,4096]{2,1,0:T(8,128)S(1)}, u32[]{:S(2)}, u32[]{:S(2)}) collective-permute-start(f32[1,32,4096]{2,1,0:T(8,128)S(1)} %get-tuple-element.11), channel_id=1, source_target_pairs={{8,0},{16,8},{24,16},{9,1},{17,9},{25,17},{10,2},{18,10},{26,18},{... | collective-permute-start | bytes 1572872 | tf_op jit(solution)/shard_map/ppermute | solution.py:17
  16.0 21.9 %copy-start.2 = (f32[3,8]{1,0:T(4,128)S(1)}, f32[3,8]{1,0:T(4,128)}, u32[]{:S(2)}) copy-start(f32[3,8]{1,0:T(4,128)} %param.3) | copy-start | bytes 292
  23.4 6.1 %copy-start = (f32[34,32,4096]{2,1,0:T(8,128)}, f32[34,32,4096]{2,1,0:T(8,128)S(1)}, u32[]{:S(2)}) copy-start(f32[34,32,4096]{2,1,0:T(8,128)S(1)} %constant_dynamic-update-slice_fusion) | copy-start | bytes 53477380
  31.4 15.2 %collective-permute-start.2 = (f32[34,1,4096]{2,1,0:T(1,128)}, f32[34,1,4096]{2,1,0:T(1,128)S(1)}, u32[]{:S(2)}, u32[]{:S(2)}) collective-permute-start(f32[34,1,4096]{2,1,0:T(1,128)} %get-tuple-element.9), channel_id=1, source_target_pairs={{1,0},{2,1},{3,2},{4,3},{5,4},{6,5},{7,6},{9,8},{10,9},{11,10},{12... | collective-permute-start | bytes 1671176 | tf_op jit(solution)/shard_map/ppermute | solution.py:17
  34.8 12.8 %collective-permute-start.3 = (f32[34,1,4096]{2,1,0:T(1,128)S(1)}, f32[34,1,4096]{2,1,0:T(1,128)S(1)}, u32[]{:S(2)}, u32[]{:S(2)}) collective-permute-start(f32[34,1,4096]{2,1,0:T(1,128)S(1)} %get-tuple-element.10), channel_id=1, source_target_pairs={{0,1},{1,2},{2,3},{3,4},{4,5},{5,6},{6,7},{8,9},{9,10},{10,11},{11... | collective-permute-start | bytes 1671176 | tf_op jit(solution)/shard_map/ppermute | solution.py:15
  47.6 0.8 copy-start.1
  173.3 23.6 %collective-permute-start.4 = (f32[4,32,2,1024]{3,2,1,0:T(2,128)S(1)}, f32[4,32,2,1024]{3,2,1,0:T(2,128)}, u32[]{:S(2)}, u32[]{:S(2)}) collective-permute-start(f32[4,32,2,1024]{3,2,1,0:T(2,128)S(1)} %bitcast.72), channel_id=1, source_target_pairs={{0,8},{8,0},{16,24},{24,16},{1,9},{9,1},{17,25},{25,17},{2,10},{10... | collective-permute-start | bytes 3145736 | tf_op jit(solution)/shard_map/ppermute | solution.py:27
  201.0 24.9 %collective-permute-start.5 = (f32[4,32,1,1024]{3,2,1,0:T(1,128)S(1)}, f32[4,32,1,1024]{3,2,1,0:T(1,128)S(1)}, u32[]{:S(2)}, u32[]{:S(2)}) collective-permute-start(f32[4,32,1,1024]{3,2,1,0:T(1,128)S(1)} %fusion.10), channel_id=1, source_target_pairs={{0,16},{8,24},{16,0},{24,8},{1,17},{9,25},{17,1},{25,9},{2,18},{10... | collective-permute-start | bytes 1572872 | tf_op jit(solution)/shard_map/ppermute | solution.py:27
where the time goes:
time: 230 us; the launch traced here: 228 us
  other arithmetic  126 us (55%)
  waiting for transfers between devices  63.7 us (28%)
  local copies, waits for them, and re-layouts  24.6 us (11%)
  starting transfers between devices  14.2 us (6%)
    another operation x1, other arithmetic, on_device(): before = jnp.cumsum(tau, axis=0) - tau  79.4 us
    ppermute x2, waiting for transfers between devices, swapped(): return lax.ppermute(value, axis, pairs)  45.9 us
    reduce_sum x1, other arithmetic, on_device(): channels = [jnp.sum(weight * c, axis=0) for c in colors]  35.3 us
    unnamed x14, local copies, waits for them, and re-layouts  17.5 us
    ppermute x2, waiting for transfers between devices, padded_2(): lax.ppermute(tail, axis, [(i, (i + 1) % count) for i in range(ends)])  10.4 us
    ppermute x2, waiting for transfers between devices, padded_2(): lax.ppermute(head, axis, [((i + 1) % count, i) for i in range(ends)])  7.36 us
    ppermute x2, starting transfers between devices, padded_2(): lax.ppermute(tail, axis, [(i, (i + 1) % count) for i in range(ends)])  6.22 us
    ppermute x2, starting transfers between devices, padded_2(): lax.ppermute(head, axis, [((i + 1) % count, i) for i in range(ends)])  5.55 us
  transfers between devices with their start and end apart: 6, of which 5 were waited for; matrix products, arithmetic and copies ran while one was open for 4% of the time, Pallas kernels for 0%

commit v1 on v0

v1 whole, which is shorter than its diff:
```python
import functools
import math

import jax
import jax.numpy as jnp
from jax import lax
from jax.experimental import pallas as pl
from jax.experimental.pallas import tpu as pltpu
from jax.sharding import PartitionSpec as P

LANES = 128
TOP = 8
LOG2E = math.log2(math.e)
MESH = pl.DeviceIdType.MESH


def kernel(
    n, m, vol, pal, out, vb, part, from_left, from_right, y_send, y_recv,
    edge_sem, body_sem, z_send_sem, z_recv_sem, y_send_sem, y_recv_sem,
    r_send_sem, r_recv_sem, l_send_sem, l_recv_sem,
):
    depth, rows, columns = vol.shape
    chunks = columns // LANES
    per = chunks // n
    pieces = 2 if per % 2 == 0 else 1
    step = per // pieces
    tiles = rows // 8
    bumps = pal.shape[1]
    me = lax.axis_index("depth")
    row = lax.axis_index("row")
    has_front, has_back = me > 0, me < n - 1
    has_up, has_down = row > 0, row < m - 1
    front, back = {"depth": me - 1}, {"depth": me + 1}
    up, down = {"row": row - 1}, {"row": row + 1}
    sides = ((has_front, front), (has_back, back), (has_up, up), (has_down, down))

    is_last = jnp.where(me == n - 1, 1, 0)

    def block_at(k):
        return is_last * k + (1 - is_last) * (n - 1 - k)

    def edge_copy(end, c):
        z = 0 if end == 0 else depth - 1
        return pltpu.make_async_copy(
            vol.at[z, :, pl.ds(pl.multiple_of(c * LANES, LANES), LANES)],
            vb.at[z + 1, c + 1, pl.ds(TOP, rows), :],
            edge_sem.at[end, c],
        )

    def body_copy(c):
        return pltpu.make_async_copy(
            vol.at[pl.ds(1, depth - 2), :, pl.ds(pl.multiple_of(c * LANES, LANES), LANES)],
            vb.at[pl.ds(2, depth - 2), c + 1, pl.ds(TOP, rows), :],
            body_sem.at[c],
        )

    @pl.loop(0, chunks)
    def _(i):
        c = block_at(i // per) * per + i % per
        edge_copy(0, c).start()
        edge_copy(1, c).start()

    @pl.loop(0, chunks)
    def _(i):
        c = block_at(i // per) * per + i % per
        body_copy(c).start()

    barrier = pltpu.get_barrier_semaphore()
    for there, device in sides:
        @pl.when(there)
        def _():
            pl.semaphore_signal(barrier, inc=1, device_id=device, device_id_type=MESH)

    zeros = jnp.zeros((8, LANES), jnp.float32)

    @pl.loop(0, depth)
    def _(z):
        for t in range(tiles):
            vb[z + 1, 0, pl.ds(TOP + 8 * t, 8), :] = zeros
            vb[z + 1, chunks + 1, pl.ds(TOP + 8 * t, 8), :] = zeros

    for missing, plane in ((me == 0, 0), (me == n - 1, depth + 1)):
        @pl.when(missing)
        def _():
            @pl.loop(0, chunks)
            def _(c):
                for t in range(tiles):
                    vb[plane, c + 1, pl.ds(TOP + 8 * t, 8), :] = zeros

    for missing, at in ((row == 0, TOP - 1), (row == m - 1, TOP + rows)):
        @pl.when(missing)
        def _():
            @pl.loop(0, depth)
            def _(z):
                for b in range(n):
                    vb[z + 1, pl.ds(1 + b * per, per), at, :] = jnp.zeros((per, LANES), jnp.float32)

    count = sum(jnp.where(there, 1, 0) for there, _ in sides)
    pl.semaphore_wait(barrier, count)

    def z_copy(way, b):
        source, target, device = (1, depth + 1, front) if way == 0 else (depth, 0, back)
        cells = (pl.ds(1 + b * per, per), pl.ds(TOP, rows))
        return pltpu.make_async_remote_copy(
            src_ref=vb.at[source, cells[0], cells[1], :],
            dst_ref=vb.at[target, cells[0], cells[1], :],
            send_sem=z_send_sem.at[way, b],
            recv_sem=z_recv_sem.at[way, b],
            device_id=device,
            device_id_type=MESH,
        )

    def y_copy(way, b):
        return pltpu.make_async_remote_copy(
            src_ref=y_send.at[way, b],
            dst_ref=y_recv.at[way, b],
            send_sem=y_send_sem.at[way, b],
            recv_sem=y_recv_sem.at[way, b],
            device_id=up if way == 0 else down,
            device_id_type=MESH,
        )

    @pl.loop(0, n)
    def _(k):
        b = block_at(k)

        @pl.loop(0, per)
        def _(i):
            edge_copy(0, b * per + i).wait()
            edge_copy(1, b * per + i).wait()

        @pl.when(has_front)
        def _():
            z_copy(0, b).start()

        @pl.when(has_back)
        def _():
            z_copy(1, b).start()

    @pl.loop(0, n)
    def _(k):
        b = block_at(k)

        @pl.loop(0, per)
        def _(i):
            body_copy(b * per + i).wait()

        here = pl.ds(1 + b * per, per)
        for way, there, at in ((0, has_up, TOP), (1, has_down, TOP + rows - 1)):
            @pl.when(there)
            def _():
                @pl.loop(0, depth)
                def _(z):
                    y_send[way, b, z] = vb[z + 1, here, at, :]

                y_copy(way, b).start()

    lane = lax.broadcasted_iota(jnp.int32, (8, LANES), 1)
    first, last = lane == 0, lane == LANES - 1
    scale = 4.0 / (depth * n)
    wide = float(bumps - 1)
    along_gain = 0.6
    gains = [
        [pal[k, j] * (along_gain * math.exp(-float(j * j))) for j in range(bumps)]
        for k in range(3)
    ]

    def pixels(c, t):
        rows_here = pl.ds(pl.multiple_of(TOP + 8 * t, 8), 8)
        rows_up = pl.ds(TOP - 1 + 8 * t, 8)
        rows_down = pl.ds(TOP + 1 + 8 * t, 8)
        before = vb[0, c + 1, rows_here, :]
        here = vb[1, c + 1, rows_here, :]
        passed = None
        sums = [None] * bumps
        for z in range(1, depth + 1):
            after = vb[z + 1, c + 1, rows_here, :]
            dz = after - before
            dy = vb[z, c + 1, rows_down, :] - vb[z, c + 1, rows_up, :]
            left = jnp.where(last, vb[z, c, rows_here, :], here)
            right = jnp.where(first, vb[z, c + 2, rows_here, :], here)
            dx = pltpu.roll(right, LANES - 1, 1) - pltpu.roll(left, 1, 1)
            along = dx + 0.45 * dz + 0.6 * dy
            square = (dx * dx + 0.16) + (dy * dy + dz * dz)
            shade = jnp.abs(along) * lax.rsqrt(square) + 0.25 / along_gain
            clear = jnp.exp2(here * (-scale * LOG2E))
            power = jnp.exp2(here * (2.0 * wide * LOG2E))
            base = jnp.exp2((here * (-wide * wide * LOG2E)) * here)
            now = clear if passed is None else passed * clear
            weight = (1.0 if passed is None else passed) - now
            passed = now
            term = (weight * base) * shade
            for j in range(bumps):
                sums[j] = term if sums[j] is None else sums[j] + term
                if j < bumps - 1:
                    term = term * power
            before, here = here, after
        for k in range(3):
            total = gains[k][0] * sums[0]
            for j in range(1, bumps):
                total = total + gains[k][j] * sums[j]
            part[c, k, pl.ds(pl.multiple_of(8 * t, 8), 8), :] = total
        part[c, 3, pl.ds(pl.multiple_of(8 * t, 8), 8), :] = passed

    def right_copy(source, b, p):
        cells = pl.ds(b * per + p * step, step)
        return pltpu.make_async_remote_copy(
            src_ref=source.at[cells],
            dst_ref=from_left.at[cells],
            send_sem=r_send_sem.at[b, p],
            recv_sem=r_recv_sem.at[b, p],
            device_id=back,
            device_id_type=MESH,
        )

    def left_copy(source, b, p):
        cells = pl.ds(b * per + p * step, step)
        return pltpu.make_async_remote_copy(
            src_ref=source.at[cells],
            dst_ref=from_right.at[cells],
            send_sem=l_send_sem.at[b, p],
            recv_sem=l_recv_sem.at[b, p],
            device_id=front,
            device_id_type=MESH,
        )

    def take_halo(b):
        @pl.when(has_front)
        def _():
            z_copy(1, b).wait_recv()

        @pl.when(has_back)
        def _():
            z_copy(0, b).wait_recv()

        here = pl.ds(1 + b * per, per)
        for way, there, at in ((1, has_up, TOP - 1), (0, has_down, TOP + rows)):
            @pl.when(there)
            def _():
                y_copy(way, b).wait_recv()

                @pl.loop(0, depth)
                def _(z):
                    vb[z + 1, here, at, :] = y_recv[way, b, z]

    @pl.loop(0, n)
    def _(k):
        b = block_at(k)
        take_halo(b)

        @pl.loop(0, pieces)
        def _(p):
            @pl.loop(0, step * tiles)
            def _(i):
                pixels(b * per + p * step + i // tiles, i % tiles)

            @pl.when((me == 0) & (b > 0))
            def _():
                right_copy(part, b, p).start()

            @pl.when((me == n - 1) & (b < n - 1))
            def _():
                left_copy(part, b, p).start()

    def blend(c, t, ahead, behind, store):
        at = pl.ds(pl.multiple_of(8 * t, 8), 8)
        passes = ahead[c, 3, at, :]
        values = [ahead[c, k, at, :] + passes * behind[c, k, at, :] for k in range(3)]
        values.append(passes * behind[c, 3, at, :])
        for k in range(4):
            store[c, k, at, :] = values[k]

    def blend_piece(b, p, ahead, behind, store):
        @pl.loop(0, step * tiles)
        def _(i):
            blend(b * per + p * step + i // tiles, i % tiles, ahead, behind, store)

    for s in range(n - 1):
        for p in range(pieces):
            b = n - 1 - s

            @pl.when((me > 0) & (me < b))
            def _():
                right_copy(part, b, p).wait_recv()
                blend_piece(b, p, from_left, part, from_left)
                right_copy(from_left, b, p).start()

            a = s

            @pl.when((me > a) & (me < n - 1))
            def _():
                left_copy(part, a, p).wait_recv()
                blend_piece(a, p, part, from_right, from_right)
                left_copy(from_right, a, p).start()

    @pl.loop(0, pieces)
    def _(p):
        @pl.when(has_front)
        def _():
            right_copy(part, me, p).wait_recv()
            blend_piece(me, p, from_left, part, part)

        @pl.when(has_back)
        def _():
            left_copy(part, me, p).wait_recv()
            blend_piece(me, p, part, from_right, part)

    @pl.loop(0, tiles)
    def _(t):
        at = pl.ds(pl.multiple_of(8 * t, 8), 8)
        for i in range(per):
            for k in range(4):
                value = part[me * per + i, k, at, :]
                out[k, at, pl.ds(i * LANES, LANES)] = 1.0 - value if k == 3 else value

    @pl.loop(0, n)
    def _(b):
        @pl.when(has_front)
        def _():
            z_copy(0, b).wait_send()

        @pl.when(has_back)
        def _():
            z_copy(1, b).wait_send()

        @pl.when(has_up)
        def _():
            y_copy(0, b).wait_send()

        @pl.when(has_down)
        def _():
            y_copy(1, b).wait_send()

        @pl.loop(0, pieces)
        def _(p):
            @pl.when(me < b)
            def _():
                right_copy(part, b, p).wait_send()

            @pl.when(me > b)
            def _():
                left_copy(part, b, p).wait_send()


def on_device(volume, palette):
    depth, rows, columns = volume.shape
    n, m = lax.axis_size("depth"), lax.axis_size("row")
    chunks = columns // LANES
    per = chunks // n
    pieces = 2 if per % 2 == 0 else 1
    image = pltpu.VMEM((chunks, 4, rows, LANES), jnp.float32)
    sides = pltpu.VMEM((2, n, depth, per, LANES), jnp.float32)
    dma = pltpu.SemaphoreType.DMA
    return pl.pallas_call(
        functools.partial(kernel, n, m),
        out_shape=jax.ShapeDtypeStruct((4, rows, columns // n), jnp.float32),
        in_specs=[
            pl.BlockSpec(memory_space=pl.ANY),
            pl.BlockSpec(memory_space=pltpu.SMEM),
        ],
        out_specs=pl.BlockSpec(memory_space=pltpu.VMEM),
        scratch_shapes=[
            pltpu.VMEM((depth + 2, chunks + 2, rows + 16, LANES), jnp.float32),
            image, image, image, sides, sides,
            dma((2, chunks)), dma((chunks,)),
            dma((2, n)), dma((2, n)), dma((2, n)), dma((2, n)),
            dma((n, pieces)), dma((n, pieces)), dma((n, pieces)), dma((n, pieces)),
        ],
        compiler_params=pltpu.CompilerParams(
            collective_id=0, has_side_effects=True, vmem_limit_bytes=56 * 2**20
        ),
    )(volume, palette)


def solution(mesh):
    return jax.shard_map(
        on_device,
        mesh=mesh,
        in_specs=(P("depth", "row", None), P()),
        out_specs=P(None, "row", "depth"),
        check_vma=False,
    )
```

time: 230 us -> 89.7 us (0.39)
  the two profiles are of different devices: /device:TPU:11 before, /device:TPU:16 now
where the time goes in v1:
time: 89.7 us; the launch traced here: 89.5 us
  Pallas kernels  87.6 us (98%)
  local copies, waits for them, and re-layouts  1.89 us (2%)
    pallas_call x1, Pallas kernels, on_device(): pl.pallas_call(functools.partial(kernel, n, m), out_shape=jax.ShapeDtypeS...  87.6 us
    unnamed x1, local copies, waits for them, and re-layouts  1.89 us

profile of v1, /device:TPU:16, one launch (start us, length us, event | category | flops | bytes accessed | tf_op | source)
XLA Modules:
  0.0 89.5 jit_solution(6625606321992854553)
XLA Ops:
  0.0 87.6 %shard_map.28 = f32[4,32,1024]{2,1,0:T(8,128)} custom-call(f32[32,32,4096]{2,1,0:T(8,128)} %vol.1, f32[3,8]{1,0:T(4,128)} %pal.1), custom_call_target="tpu_custom_call" | custom-call | tf_op jit(solution)/shard_map/pallas_call | solution.py:354
  87.6 1.9 %copy.4 = f32[4,32,1024]{2,1,0:T(8,128)} copy(f32[4,32,1024]{2,1,0:T(8,128)} %shard_map.28) | data formatting | bytes 1048576

commit v2 on v1

--- a/solution.py
+++ b/solution.py
@@ -34,10 +34,12 @@
     up, down = {"row": row - 1}, {"row": row + 1}
     sides = ((has_front, front), (has_back, back), (has_up, up), (has_down, down))
 
-    is_last = jnp.where(me == n - 1, 1, 0)
+    def block_of(device, k):
+        rising = jnp.where(device >= n // 2, 1, 0)
+        return rising * k + (1 - rising) * (n - 1 - k)
 
     def block_at(k):
-        return is_last * k + (1 - is_last) * (n - 1 - k)
+        return block_of(me, k)
 
     def edge_copy(end, c):
         z = 0 if end == 0 else depth - 1
@@ -120,26 +122,22 @@
             device_id_type=MESH,
         )
 
+    @pl.loop(0, chunks)
+    def _(c):
+        edge_copy(0, c).wait()
+        edge_copy(1, c).wait()
+
     @pl.loop(0, n)
     def _(k):
         b = block_at(k)
 
-        @pl.loop(0, per)
-        def _(i):
-            edge_copy(0, b * per + i).wait()
-            edge_copy(1, b * per + i).wait()
-
         @pl.when(has_front)
         def _():
-            z_copy(0, b).start()
+            z_copy(0, block_of(me - 1, k)).start()
 
         @pl.when(has_back)
         def _():
-            z_copy(1, b).start()
-
-    @pl.loop(0, n)
-    def _(k):
-        b = block_at(k)
+            z_copy(1, block_of(me + 1, k)).start()
 
         @pl.loop(0, per)
         def _(i):
@@ -243,25 +241,6 @@
                 def _(z):
                     vb[z + 1, here, at, :] = y_recv[way, b, z]
 
-    @pl.loop(0, n)
-    def _(k):
-        b = block_at(k)
-        take_halo(b)
-
-        @pl.loop(0, pieces)
-        def _(p):
-            @pl.loop(0, step * tiles)
-            def _(i):
-                pixels(b * per + p * step + i // tiles, i % tiles)
-
-            @pl.when((me == 0) & (b > 0))
-            def _():
-                right_copy(part, b, p).start()
-
-            @pl.when((me == n - 1) & (b < n - 1))
-            def _():
-                left_copy(part, b, p).start()
-
     def blend(c, t, ahead, behind, store):
         at = pl.ds(pl.multiple_of(8 * t, 8), 8)
         passes = ahead[c, 3, at, :]
@@ -275,23 +254,53 @@
         def _(i):
             blend(b * per + p * step + i // tiles, i % tiles, ahead, behind, store)
 
-    for s in range(n - 1):
-        for p in range(pieces):
-            b = n - 1 - s
-
-            @pl.when((me > 0) & (me < b))
+    def render(k):
+        b = block_at(k)
+        take_halo(b)
+
+        @pl.loop(0, pieces)
+        def _(p):
+            @pl.loop(0, step * tiles)
+            def _(i):
+                pixels(b * per + p * step + i // tiles, i % tiles)
+
+            @pl.when((me == 0) & (b > 0))
+            def _():
+                right_copy(part, b, p).start()
+
+            @pl.when((me == n - 1) & (b < n - 1))
+            def _():
+                left_copy(part, b, p).start()
+
+    def pass_on(turn):
+        b = n - 1 - turn + me
+        a = turn - (n - 1) + me
+
+        @pl.loop(0, pieces)
+        def _(p):
+            @pl.when((me > 0) & (me < b) & (b < n))
             def _():
                 right_copy(part, b, p).wait_recv()
                 blend_piece(b, p, from_left, part, from_left)
                 right_copy(from_left, b, p).start()
 
-            a = s
-
-            @pl.when((me > a) & (me < n - 1))
+            @pl.when((me < n - 1) & (a >= 0) & (a < me))
             def _():
                 left_copy(part, a, p).wait_recv()
                 blend_piece(a, p, part, from_right, from_right)
                 left_copy(from_right, a, p).start()
+
+    @pl.loop(0, n)
+    def _(k):
+        render(k)
+
+        @pl.when(k == max(n - 2, 0))
+        def _():
+            pass_on(1)
+
+    @pl.loop(2, max(n - 1, 2))
+    def _(turn):
+        pass_on(turn)
 
     @pl.loop(0, pieces)
     def _(p):

time: 89.7 us -> 63.3 us (0.71)
  the two profiles are of different devices: /device:TPU:16 before, /device:TPU:11 now
where the time goes in v2:
time: 63.3 us; the launch traced here: 63.1 us
  Pallas kernels  61.2 us (97%)
  local copies, waits for them, and re-layouts  1.89 us (3%)
    pallas_call x1, Pallas kernels, on_device(): pl.pallas_call(functools.partial(kernel, n, m), out_shape=jax.ShapeDtypeS...  61.2 us
    unnamed x1, local copies, waits for them, and re-layouts  1.89 us

profile of v2, /device:TPU:11, one launch (start us, length us, event | category | flops | bytes accessed | tf_op | source)
XLA Modules:
  0.0 63.1 jit_solution(10500683394923623356)
XLA Ops:
  0.0 61.2 %shard_map.28 = f32[4,32,1024]{2,1,0:T(8,128)} custom-call(f32[32,32,4096]{2,1,0:T(8,128)} %vol.1, f32[3,8]{1,0:T(4,128)} %pal.1), custom_call_target="tpu_custom_call" | custom-call | tf_op jit(solution)/shard_map/pallas_call | solution.py:363
  61.2 1.9 %copy.4 = f32[4,32,1024]{2,1,0:T(8,128)} copy(f32[4,32,1024]{2,1,0:T(8,128)} %shard_map.28) | data formatting | bytes 1048576

commit v3 on v2

--- a/solution.py
+++ b/solution.py
@@ -22,7 +22,7 @@
     depth, rows, columns = vol.shape
     chunks = columns // LANES
     per = chunks // n
-    pieces = 2 if per % 2 == 0 else 1
+    pieces = 4 if per % 4 == 0 else 1
     step = per // pieces
     tiles = rows // 8
     bumps = pal.shape[1]
@@ -127,17 +127,17 @@
         edge_copy(0, c).wait()
         edge_copy(1, c).wait()
 
-    @pl.loop(0, n)
-    def _(k):
+    def send_planes(k):
+        @pl.when(has_front)
+        def _():
+            z_copy(0, block_of(me - 1, k)).start()
+
+        @pl.when(has_back)
+        def _():
+            z_copy(1, block_of(me + 1, k)).start()
+
+    def send_rows(k):
         b = block_at(k)
-
-        @pl.when(has_front)
-        def _():
-            z_copy(0, block_of(me - 1, k)).start()
-
-        @pl.when(has_back)
-        def _():
-            z_copy(1, block_of(me + 1, k)).start()
 
         @pl.loop(0, per)
         def _(i):
@@ -152,6 +152,17 @@
                     y_send[way, b, z] = vb[z + 1, here, at, :]
 
                 y_copy(way, b).start()
+
+    ahead_blocks = min(2, n)
+
+    @pl.loop(0, ahead_blocks)
+    def _(k):
+        send_planes(k)
+        send_rows(k)
+
+    @pl.loop(ahead_blocks, n)
+    def _(k):
+        send_planes(k)
 
     lane = lax.broadcasted_iota(jnp.int32, (8, LANES), 1)
     first, last = lane == 0, lane == LANES - 1
@@ -294,6 +305,10 @@
     def _(k):
         render(k)
 
+        @pl.when(k + ahead_blocks < n)
+        def _():
+            send_rows(k + ahead_blocks)
+
         @pl.when(k == max(n - 2, 0))
         def _():
             pass_on(1)
@@ -356,7 +371,7 @@
     n, m = lax.axis_size("depth"), lax.axis_size("row")
     chunks = columns // LANES
     per = chunks // n
-    pieces = 2 if per % 2 == 0 else 1
+    pieces = 4 if per % 4 == 0 else 1
     image = pltpu.VMEM((chunks, 4, rows, LANES), jnp.float32)
     sides = pltpu.VMEM((2, n, depth, per, LANES), jnp.float32)
     dma = pltpu.SemaphoreType.DMA

time: 63.3 us -> 64.7 us (1.022)
  Pallas kernels: 61.2 us -> 62.7 us
    pallas_call x1, Pallas kernels: 61.2 us -> 62.7 us  [on_device(): pl.pallas_call(functools.partial(kernel, n, m), out_shape=jax.ShapeDtypeS...]
where the time goes in v3:
time: 64.7 us; the launch traced here: 64.6 us
  Pallas kernels  62.7 us (97%)
  local copies, waits for them, and re-layouts  1.89 us (3%)
    pallas_call x1, Pallas kernels, on_device(): pl.pallas_call(functools.partial(kernel, n, m), out_shape=jax.ShapeDtypeS...  62.7 us
    unnamed x1, local copies, waits for them, and re-layouts  1.89 us

profile of v3, /device:TPU:11, one launch (start us, length us, event | category | flops | bytes accessed | tf_op | source)
XLA Modules:
  0.0 64.6 jit_solution(4320601598533004698)
XLA Ops:
  0.0 62.7 %shard_map.28 = f32[4,32,1024]{2,1,0:T(8,128)} custom-call(f32[32,32,4096]{2,1,0:T(8,128)} %vol.1, f32[3,8]{1,0:T(4,128)} %pal.1), custom_call_target="tpu_custom_call" | custom-call | tf_op jit(solution)/shard_map/pallas_call | solution.py:378
  62.7 1.9 %copy.4 = f32[4,32,1024]{2,1,0:T(8,128)} copy(f32[4,32,1024]{2,1,0:T(8,128)} %shard_map.28) | data formatting | bytes 1048576
